TPU v7x, 128 devices: a whole 4x4x4 slice. The times are simulated.
128 devices in a mesh: row: 8 (over y_hi, x), feat: 16 (over y_lo, z, core).
Axes of the slice: x: 4, y: 4 (y_hi: 2, y_lo: 2; y = y_hi * 2 + y_lo), z: 4, core: 2. Of those that a mesh axis runs over, the one named last changes fastest.
Arguments:
- design_tiles: bfloat16 [8, 8, 8, 48, 128, 128], P('row', None, None, 'feat'), may hold values from -0.078125 to 0.078125
- block_ids: int32 [8, 8, 8, 48], P(None, None, None, 'feat'), may hold values from 0 to 1023, as said below
- responses: bfloat16 [8, 8, 8, 128, 64], P('row'), may hold values from -6 to 6
- live_groups: int32 [8, 8], replicated, may hold values from 0 to 1, as said below
- start_coef: float32 [131072, 64], P('feat'), may hold values from -6 to 6
Outputs:
- coefficients: float32 [131072, 64], P('feat')
Inputs may be any that keep to these rules, and one draw needn't show every extreme that they name: `block_ids`: the 3 entries of a row block that lie in feat index f's positions are distinct feature blocks of the range f * 64 to (f + 1) * 64 - 1. `live_groups`: A group is all live or all empty; every owner has live groups from exactly half of the 8 sources.
All inputs are finite; a program needn't handle non-finite values.
Results may differ from a plain program's by a relative error of at most 0.002.
Values may be sent and summed in bfloat16 or wider, within the bound.
No kernel may reach another device: no remote copies, remote signals or barrier semaphores. Data moves between devices by JAX's collectives and lax.ppermute only.
A program may use at most 64 MiB of HBM per device.

v0:
```python
import jax
import jax.numpy as jnp
from jax import lax
from jax.sharding import PartitionSpec as P

ITERS = 2
step_size = 0.25
ridge_term = 0.05


def huber_weights(predicted, work_resp, live_flags):
    groups, slot_count, block_rows, columns = predicted.shape
    threshold = 1.4 * columns**0.5
    totals = lax.psum(predicted, "feat")
    residual = work_resp.astype(jnp.float32) - totals
    row_norms = jnp.sqrt(jnp.sum(residual * residual, axis=-1))
    weight = live_flags[:, None, None] * threshold / jnp.maximum(row_norms, threshold)
    scaled = (weight[..., None] * residual).astype(jnp.bfloat16)
    return (scaled, weight.astype(jnp.bfloat16))


def body(design_tiles, block_ids, responses, live_groups, start_coef):
    row_place = lax.axis_index("row")
    feat_place = lax.axis_index("feat")
    block_width = design_tiles.shape[-1]
    columns = start_coef.shape[1]
    local_blocks = start_coef.shape[0] // block_width
    local_ids = block_ids - feat_place * local_blocks
    work_tiles = design_tiles[0]
    work_resp = responses[0]
    work_ids = lax.dynamic_index_in_dim(local_ids, row_place, 0, keepdims=False)
    live_flags = lax.dynamic_index_in_dim(live_groups, row_place, 0, keepdims=False).astype(
        jnp.float32
    )
    onehot = (
        work_ids.reshape(-1)[:, None] == jnp.arange(local_blocks, dtype=jnp.int32)[None, :]
    ).astype(jnp.float32)
    tiles_wide = work_tiles.astype(jnp.float32)
    tile_squares = tiles_wide * tiles_wide
    coefficients = start_coef
    for iteration in range(ITERS):
        coef_bf = coefficients.astype(jnp.bfloat16).reshape(local_blocks, block_width, columns)
        picked = coef_bf[work_ids]
        predicted = jnp.einsum(
            "gskif,gskfc->gsic", work_tiles, picked, preferred_element_type=jnp.float32
        )
        scaled, rounded = huber_weights(predicted, work_resp, live_flags)
        partial_grad = jnp.einsum(
            "gskif,gsic->gskfc", work_tiles, scaled, preferred_element_type=jnp.float32
        )
        partial_curv = jnp.einsum(
            "gskif,gsi->gskf",
            tile_squares,
            rounded.astype(jnp.float32),
            precision=lax.Precision.HIGHEST,
        )
        gradient = jnp.einsum(
            "tb,tfc->bfc",
            onehot,
            partial_grad.reshape(-1, block_width, columns),
            precision=lax.Precision.HIGHEST,
        )
        curvature = jnp.einsum(
            "tb,tf->bf",
            onehot,
            partial_curv.reshape(-1, block_width),
            precision=lax.Precision.HIGHEST,
        )
        gradient, curvature = lax.psum((gradient, curvature), "row")
        coefficients = coefficients + step_size * (
            gradient.reshape(-1, columns) - ridge_term * coefficients
        ) / (curvature.reshape(-1, 1) + ridge_term)
    return coefficients


def solution(mesh):
    in_specs = (
        P("row", None, None, "feat", None, None),
        P(None, None, None, "feat"),
        P("row", None, None, None, None),
        P(),
        P("feat", None),
    )
    out_specs = P("feat", None)
    return jax.shard_map(body, mesh=mesh, in_specs=in_specs, out_specs=out_specs, check_vma=False)
```

profile of v0, /device:TPU:0, one launch (start us, length us, event | category | flops | bytes accessed | tf_op | source)
XLA Modules:
  0.0 509.8 jit_solution(7656828350380415054)
XLA Ops:
  6.5 0.7 compare_select_fusion
  7.4 0.1 reshape.107
  7.5 1.9 copy_bitcast_fusion.3
  9.4 2.7 gather_fusion
  12.1 8.0 %fusion.16 = f32[8,8,128,64]{2,3,1,0:T(8,128)} fusion(bf16[8,8,3,128,64]{3,4,2,1,0:T(8,128)(2,1)} %bitcast.118, bf16[1,8,8,3,128,128]{5,4,3,2,1,0:T(8,128)(2,1)} %param.5), kind=kOutput, calls=%fused_computation.29 | convolution fusion | flops 402653184 | bytes 11534336 | tf_op jit(solution)/shard_map/gskif,gskfc->gsic/dot_general | solution.py:44
  20.1 0.2 all-reduce.7.cloned.1.call-start
  20.5 0.1 eq.15
  20.6 0.7 multiply_bitcast_fusion
  21.3 124.6 %all-reduce.5.cloned.1.call-done = f32[8,8,128,64]{2,3,1,0:T(8,128)} async-done(((f32[8,8,128,64]{2,3,1,0:T(8,128)}), f32[8,8,128,64]{2,3,1,0:T(8,128)}) %all-reduce.5.cloned.1.call-update) | async-done | bytes 2097168 | tf_op jit(solution)/shard_map/psum | solution.py:14
  146.0 2.2 multiply_reduce_fusion.1
  148.2 4.1 fusion.8
  152.3 6.2 %fusion.14 = f32[64,128,64]{1,0,2:T(8,128)S(1)} fusion(f32[192,128,64]{1,2,0:T(8,128)S(1)} %bitcast.115, s32[192]{0:T(256)S(1)} %eq.15), kind=kOutput, calls=%fused_computation.17 | convolution fusion | flops 1207971840 | bytes 8389376 | tf_op jit(solution)/shard_map/tb,tfc->bfc/dot_general | solution.py:57
  158.5 2.5 copy.46
  161.1 0.3 all-reduce.9.cloned.1.call-start
  161.3 7.4 %fusion.1 = f32[8,8,1,3,128]{4,2,3,1,0:T(1,128)S(1)} fusion(bf16[1,8,8,3,128,128]{5,4,3,2,1,0:T(8,128)(2,1)} %param.5, bf16[8,8,128,1,1]{2,1,0,3,4:T(8,128)(2,1)S(1)} %get-tuple-element.7), kind=kOutput, calls=%fused_computation.4 | convolution fusion | flops 44040192 | bytes 6406144 | tf_op jit(solution)/shard_map/gskif,gsi->gskf/dot_general | solution.py:51
  168.8 0.2 fusion.31
  169.0 41.4 %psum.44 = f32[64,128]{1,0:T(8,128)S(1)} all-reduce(f32[64,128]{1,0:T(8,128)S(1)} %fusion.31), channel_id=1, replica_groups=mesh['row'=8,'feat'=16] {'row'}, use_global_device_ids=true, to_apply=%region_3.4 | all-reduce | flops 8192 | bytes 65536 | tf_op jit(solution)/shard_map/psum | solution.py:69
  210.4 44.2 %all-reduce.7.cloned.1.call-done = f32[8192,64]{0,1:T(8,128)} async-done(((f32[8192,64]{0,1:T(8,128)}), f32[8192,64]{0,1:T(8,128)}) %all-reduce.7.cloned.1.call-update) | async-done | bytes 2097168 | tf_op jit(solution)/shard_map/psum | solution.py:69
  254.6 2.7 copy_bitcast_fusion.2
  257.3 2.7 gather_fusion.1
  260.0 8.0 %fusion.19 = f32[8,8,128,64]{2,3,1,0:T(8,128)} fusion(bf16[8,8,3,128,64]{3,4,2,1,0:T(8,128)(2,1)} %bitcast.117, bf16[1,8,8,3,128,128]{5,4,3,2,1,0:T(8,128)(2,1)} %param.5), kind=kOutput, calls=%fused_computation.30 | convolution fusion | flops 402653184 | bytes 11534336 | tf_op jit(solution)/shard_map/gskif,gskfc->gsic/dot_general | solution.py:44
  268.0 0.3 all-reduce.11.cloned.1.call-start
  268.3 122.0 %all-reduce.9.cloned.1.call-done = f32[8,8,128,64]{2,3,1,0:T(8,128)} async-done(((f32[8,8,128,64]{2,3,1,0:T(8,128)}), f32[8,8,128,64]{2,3,1,0:T(8,128)}) %all-reduce.9.cloned.1.call-update) | async-done | bytes 2097168 | tf_op jit(solution)/shard_map/psum | solution.py:14
  390.3 2.2 multiply_reduce_fusion
  392.5 4.1 fusion.3
  396.6 6.2 %fusion.12 = f32[64,128,64]{1,0,2:T(8,128)S(1)} fusion(f32[192,128,64]{1,2,0:T(8,128)S(1)} %bitcast.116, s32[192]{0:T(256)S(1)} %eq.15), kind=kOutput, calls=%fused_computation.15 | convolution fusion | flops 1207971840 | bytes 8389376 | tf_op jit(solution)/shard_map/tb,tfc->bfc/dot_general | solution.py:57
  402.8 2.5 copy.45
  405.4 7.8 %fusion = f32[8,8,1,3,128]{4,2,3,1,0:T(1,128)S(1)} fusion(bf16[1,8,8,3,128,128]{5,4,3,2,1,0:T(8,128)(2,1)} %param.5, bf16[8,8,128,1,1]{2,1,0,3,4:T(8,128)(2,1)S(1)} %get-tuple-element.5), kind=kOutput, calls=%fused_computation.3 | convolution fusion | flops 44040192 | bytes 6406144 | tf_op jit(solution)/shard_map/gskif,gsi->gskf/dot_general | solution.py:51
  413.3 0.2 fusion.30
  413.5 41.4 %psum.47 = f32[64,128]{1,0:T(8,128)S(1)} all-reduce(f32[64,128]{1,0:T(8,128)S(1)} %fusion.30), channel_id=1, replica_groups=mesh['row'=8,'feat'=16] {'row'}, use_global_device_ids=true, to_apply=%region_7.8 | all-reduce | flops 8192 | bytes 65536 | tf_op jit(solution)/shard_map/psum | solution.py:69
  454.9 44.2 %all-reduce.11.cloned.1.call-done = f32[8192,64]{0,1:T(8,128)} async-done(((f32[8192,64]{0,1:T(8,128)}), f32[8192,64]{0,1:T(8,128)}) %all-reduce.11.cloned.1.call-update) | async-done | bytes 2097168 | tf_op jit(solution)/shard_map/psum | solution.py:69
  499.1 4.2 divide_add_fusion
  (24 shorter events, 0.7 us)
Async XLA Ops:
  6.5 139.4 %all-reduce.5.cloned.1.call-start = ((), (), s32[]{:S(2)}) async-start(), calls=%async_computation | async-start | bytes 4194304 | tf_op jit(solution)/shard_map/psum | solution.py:14
  20.1 125.9 %copy-start = (bf16[1,8,8,128,64]{3,4,2,1,0:T(8,128)(2,1)S(1)}, bf16[1,8,8,128,64]{3,4,2,1,0:T(8,128)(2,1)}, u32[]{:S(2)}) copy-start(bf16[1,8,8,128,64]{3,4,2,1,0:T(8,128)(2,1)} %param.7) | copy-start | bytes 3145732
  20.1 234.5 %all-reduce.7.cloned.1.call-start = ((), (), s32[]{:S(2)}) async-start(), calls=%async_computation.1 | async-start | bytes 4194304 | tf_op jit(solution)/shard_map/psum | solution.py:69
  146.0 2.3 copy-start.2
  161.1 229.2 %all-reduce.9.cloned.1.call-start = ((), (), s32[]{:S(2)}) async-start(), calls=%async_computation.2 | async-start | bytes 4194304 | tf_op jit(solution)/shard_map/psum | solution.py:14
  268.0 231.1 %all-reduce.11.cloned.1.call-start = ((), (), s32[]{:S(2)}) async-start(), calls=%async_computation.3 | async-start | bytes 4194304 | tf_op jit(solution)/shard_map/psum | solution.py:69
  390.3 2.3 copy-start.3
  405.4 93.7 %copy-start.1 = (f32[8192,64]{0,1:T(8,128)S(1)}, f32[8192,64]{0,1:T(8,128)}, u32[]{:S(2)}) copy-start(f32[8192,64]{0,1:T(8,128)} %param.9) | copy-start | bytes 6291460
Sparse Core Ops, SparseCore 0:
  20.2 125.6 all-reduce.4
  161.2 93.3 all-reduce.6
  268.1 122.1 all-reduce.8
  405.5 93.5 all-reduce.10
where the time goes:
time: 510 us
  waiting for transfers between devices  335 us (66%)
  blocking collectives  82.7 us (16%)
  matrix products  52.1 us (10%)
  other arithmetic  14.8 us (3%)
  between operations  13.2 us (3%)
  local copies, waits for them, and re-layouts  11.2 us (2%)
    psum x2, waiting for transfers between devices, huber_weights(): totals = lax.psum(predicted, 'feat')  247 us
    psum x2, waiting for transfers between devices, body(): gradient, curvature = lax.psum((gradient, curvature), 'row')  88.4 us
    psum x2, blocking collectives, body(): gradient, curvature = lax.psum((gradient, curvature), 'row')  82.7 us
    dot_general x2, matrix products, body(): jnp.einsum('gskif,gskfc->gsic', work_tiles, picked, preferred_element_typ...  15.9 us
    dot_general x2, matrix products, body(): jnp.einsum('gskif,gsi->gskf', tile_squares, rounded.astype(jnp.float32),...  15.2 us
    dot_general x2, matrix products, body(): jnp.einsum('tb,tfc->bfc', onehot, partial_grad.reshape(-1, block_width, c...  12.4 us
  transfers between devices with their start and end apart: 4, of which 4 were waited for; matrix products, arithmetic and copies ran while one was open for 3% of the time, Pallas kernels for 0%

commit v1 on v0

--- a/solution.py
+++ b/solution.py
@@ -8,10 +8,15 @@
 ridge_term = 0.05
 
 
+def add_all(x, mesh_axis):
+    parts = lax.all_gather(x, mesh_axis)
+    return jnp.sum(parts, axis=0)
+
+
 def huber_weights(predicted, work_resp, live_flags):
     groups, slot_count, block_rows, columns = predicted.shape
     threshold = 1.4 * columns**0.5
-    totals = lax.psum(predicted, "feat")
+    totals = add_all(predicted, "feat")
     residual = work_resp.astype(jnp.float32) - totals
     row_norms = jnp.sqrt(jnp.sum(residual * residual, axis=-1))
     weight = live_flags[:, None, None] * threshold / jnp.maximum(row_norms, threshold)

time: 510 us -> 632 us (1.24)
  waiting for transfers between devices: 335 us -> 430 us
  other arithmetic: 14.8 us -> 41.6 us
    all_gather x0 -> x2, waiting for transfers between devices: none -> 341 us  [add_all(): parts = lax.all_gather(x, mesh_axis)]
    psum x2 -> x0, waiting for transfers between devices: 247 us -> none  [huber_weights(): totals = lax.psum(predicted, 'feat')]
    reduce_sum x0 -> x2, other arithmetic: none -> 26.9 us  [add_all(): return jnp.sum(parts, axis=0)]
where the time goes in v1:
time: 632 us
  waiting for transfers between devices  430 us (68%)
  blocking collectives  83.3 us (13%)
  matrix products  52.1 us (8%)
  other arithmetic  41.6 us (7%)
  between operations  13.2 us (2%)
  local copies, waits for them, and re-layouts  11.2 us (2%)
    all_gather x2, waiting for transfers between devices, add_all(): parts = lax.all_gather(x, mesh_axis)  341 us
    psum x2, waiting for transfers between devices, body(): gradient, curvature = lax.psum((gradient, curvature), 'row')  88 us
    psum x2, blocking collectives, body(): gradient, curvature = lax.psum((gradient, curvature), 'row')  83.3 us
    reduce_sum x2, other arithmetic, add_all(): return jnp.sum(parts, axis=0)  26.9 us
    dot_general x2, matrix products, body(): jnp.einsum('gskif,gskfc->gsic', work_tiles, picked, preferred_element_typ...  15.9 us
    dot_general x2, matrix products, body(): jnp.einsum('gskif,gsi->gskf', tile_squares, rounded.astype(jnp.float32),...  15.2 us
  transfers between devices with their start and end apart: 4, of which 4 were waited for; matrix products, arithmetic and copies ran while one was open for 3% of the time, Pallas kernels for 0%

profile of v1, /device:TPU:0, one launch (start us, length us, event | category | flops | bytes accessed | tf_op | source)
XLA Modules:
  0.0 631.8 jit_solution(385102591174954676)
XLA Ops:
  6.5 0.7 compare_select_fusion
  7.5 1.9 copy_bitcast_fusion.3
  9.4 2.7 gather_fusion
  12.1 8.0 %fusion.16 = f32[8,8,128,64]{2,3,1,0:T(8,128)} fusion(bf16[8,8,3,128,64]{3,4,2,1,0:T(8,128)(2,1)} %bitcast.122, bf16[1,8,8,3,128,128]{5,4,3,2,1,0:T(8,128)(2,1)} %param.5), kind=kOutput, calls=%fused_computation.29 | convolution fusion | flops 402653184 | bytes 11534336 | tf_op jit(solution)/shard_map/gskif,gskfc->gsic/dot_general | solution.py:49
  20.1 0.2 all-reduce.3.cloned.1.call-start
  20.6 0.7 multiply_bitcast_fusion
  21.3 172.1 %all-gather.5.cloned.1.call-done = f32[128,8,128,64]{2,3,1,0:T(8,128)} async-done(((f32[8,8,128,64]{2,3,1,0:T(8,128)}), f32[128,8,128,64]{2,3,1,0:T(8,128)}) %all-gather.5.cloned.1.call-update) | async-done | bytes 33554448 | tf_op jit(solution)/shard_map/all_gather | solution.py:12
  193.4 13.5 %reduce_sum.36 = f32[8,8,128,64]{2,3,1,0:T(8,128)} reduce(f32[16,8,8,128,64]{3,4,2,1,0:T(8,128)} %bitcast.119, f32[]{:T(128)} %constant.17.clone.1), dimensions={0}, to_apply=%region_0.1 | reduce | flops 7864320 | bytes 35651588 | tf_op jit(solution)/shard_map/reduce_sum | solution.py:13
  206.9 2.2 multiply_reduce_fusion.1
  209.1 4.1 fusion.8
  213.2 6.2 fusion.14
  219.4 2.5 copy.52
  222.0 0.3 all-gather.7.cloned.1.call-start
  222.2 7.4 %fusion.1 = f32[8,8,1,3,128]{4,2,3,1,0:T(1,128)S(1)} fusion(bf16[1,8,8,3,128,128]{5,4,3,2,1,0:T(8,128)(2,1)} %param.5, bf16[8,8,128,1,1]{2,1,0,3,4:T(8,128)(2,1)S(1)} %get-tuple-element.7), kind=kOutput, calls=%fused_computation.4 | convolution fusion | flops 44040192 | bytes 6406144 | tf_op jit(solution)/shard_map/gskif,gsi->gskf/dot_general | solution.py:56
  229.7 0.2 fusion.31
  229.9 41.7 %psum.29 = f32[64,128]{1,0:T(8,128)S(1)} all-reduce(f32[64,128]{1,0:T(8,128)S(1)} %fusion.31), channel_id=1, replica_groups=mesh['row'=8,'feat'=16] {'row'}, use_global_device_ids=true, to_apply=%region_3.4 | all-reduce | flops 8192 | bytes 65536 | tf_op jit(solution)/shard_map/psum | solution.py:74
  271.6 44.1 %all-reduce.3.cloned.1.call-done = f32[8192,64]{0,1:T(8,128)} async-done(((f32[8192,64]{0,1:T(8,128)}), f32[8192,64]{0,1:T(8,128)}) %all-reduce.3.cloned.1.call-update) | async-done | bytes 2097168 | tf_op jit(solution)/shard_map/psum | solution.py:74
  315.7 2.7 copy_bitcast_fusion.2
  318.4 2.7 gather_fusion.1
  321.1 8.0 %fusion.19 = f32[8,8,128,64]{2,3,1,0:T(8,128)} fusion(bf16[8,8,3,128,64]{3,4,2,1,0:T(8,128)(2,1)} %bitcast.121, bf16[1,8,8,3,128,128]{5,4,3,2,1,0:T(8,128)(2,1)} %param.5), kind=kOutput, calls=%fused_computation.30 | convolution fusion | flops 402653184 | bytes 11534336 | tf_op jit(solution)/shard_map/gskif,gskfc->gsic/dot_general | solution.py:49
  329.1 0.3 all-reduce.5.cloned.1.call-start
  329.4 169.4 %all-gather.7.cloned.1.call-done = f32[128,8,128,64]{2,3,1,0:T(8,128)} async-done(((f32[8,8,128,64]{2,3,1,0:T(8,128)}), f32[128,8,128,64]{2,3,1,0:T(8,128)}) %all-gather.7.cloned.1.call-update) | async-done | bytes 33554448 | tf_op jit(solution)/shard_map/all_gather | solution.py:12
  498.8 13.4 %reduce_sum.38 = f32[8,8,128,64]{2,3,1,0:T(8,128)} reduce(f32[16,8,8,128,64]{3,4,2,1,0:T(8,128)} %bitcast.120, f32[]{:T(128)} %constant.17.clone.1), dimensions={0}, to_apply=%region_4.5 | reduce | flops 7864320 | bytes 35651588 | tf_op jit(solution)/shard_map/reduce_sum | solution.py:13
  512.2 2.2 multiply_reduce_fusion
  514.5 4.1 fusion.3
  518.6 6.2 fusion.12
  524.8 2.5 copy.51
  527.3 7.8 %fusion = f32[8,8,1,3,128]{4,2,3,1,0:T(1,128)S(1)} fusion(bf16[1,8,8,3,128,128]{5,4,3,2,1,0:T(8,128)(2,1)} %param.5, bf16[8,8,128,1,1]{2,1,0,3,4:T(8,128)(2,1)S(1)} %get-tuple-element.5), kind=kOutput, calls=%fused_computation.3 | convolution fusion | flops 44040192 | bytes 6406144 | tf_op jit(solution)/shard_map/gskif,gsi->gskf/dot_general | solution.py:56
  535.3 0.2 fusion.30
  535.5 41.7 %psum.31 = f32[64,128]{1,0:T(8,128)S(1)} all-reduce(f32[64,128]{1,0:T(8,128)S(1)} %fusion.30), channel_id=1, replica_groups=mesh['row'=8,'feat'=16] {'row'}, use_global_device_ids=true, to_apply=%region_7.8 | all-reduce | flops 8192 | bytes 65536 | tf_op jit(solution)/shard_map/psum | solution.py:74
  577.1 43.9 %all-reduce.5.cloned.1.call-done = f32[8192,64]{0,1:T(8,128)} async-done(((f32[8192,64]{0,1:T(8,128)}), f32[8192,64]{0,1:T(8,128)}) %all-reduce.5.cloned.1.call-update) | async-done | bytes 2097168 | tf_op jit(solution)/shard_map/psum | solution.py:74
  621.0 4.2 divide_add_fusion
  (26 shorter events, 0.9 us)
Async XLA Ops:
  6.5 186.8 %all-gather.5.cloned.1.call-start = ((), (), s32[]{:S(2)}) async-start(), calls=%async_computation.2 | async-start | bytes 35651584 | tf_op jit(solution)/shard_map/all_gather | solution.py:12
  20.1 295.6 %all-reduce.3.cloned.1.call-start = ((), (), s32[]{:S(2)}) async-start(), calls=%async_computation | async-start | bytes 4194304 | tf_op jit(solution)/shard_map/psum | solution.py:74
  193.4 13.5 %copy-start = (bf16[1,8,8,128,64]{3,4,2,1,0:T(8,128)(2,1)S(1)}, bf16[1,8,8,128,64]{3,4,2,1,0:T(8,128)(2,1)}, u32[]{:S(2)}) copy-start(bf16[1,8,8,128,64]{3,4,2,1,0:T(8,128)(2,1)} %param.7) | copy-start | bytes 3145732
  206.9 2.3 copy-start.2
  222.0 276.9 %all-gather.7.cloned.1.call-start = ((), (), s32[]{:S(2)}) async-start(), calls=%async_computation.3 | async-start | bytes 35651584 | tf_op jit(solution)/shard_map/all_gather | solution.py:12
  329.1 291.9 %all-reduce.5.cloned.1.call-start = ((), (), s32[]{:S(2)}) async-start(), calls=%async_computation.1 | async-start | bytes 4194304 | tf_op jit(solution)/shard_map/psum | solution.py:74
  512.2 2.3 copy-start.1
  527.3 93.7 %copy-start.3 = (f32[8192,64]{0,1:T(8,128)S(1)}, f32[8192,64]{0,1:T(8,128)}, u32[]{:S(2)}) copy-start(f32[8192,64]{0,1:T(8,128)} %param.9) | copy-start | bytes 6291460
Sparse Core Ops, SparseCore 0:
  20.2 173.0 all-gather.4
  222.1 93.5 all-reduce.2
  329.2 169.5 all-gather.6
  527.4 93.5 all-reduce.4
